TPU v7x, 256 devices: a whole 4x4x8 slice. The times are simulated.
256 devices in a mesh: dp: 32 (over z, y_hi, core), ctx: 8 (over x, y_lo).
Axes of the slice: x: 4, y: 4 (y_hi: 2, y_lo: 2; y = y_hi * 2 + y_lo), z: 8, core: 2. Of those that a mesh axis runs over, the one named last changes fastest.
Arguments:
- q_heads: bfloat16 [32, 1536, 2048], P('dp', 'ctx'), may hold values from -8 to 8
- keys: bfloat16 [32, 1536, 128], P('dp', 'ctx'), may hold values from -8 to 8
- values: bfloat16 [32, 1536, 128], P('dp', 'ctx'), may hold values from -6 to 6
- out_grad: bfloat16 [32, 1536, 2048], P('dp', 'ctx'), may hold values from -0.29882812 to 0.29882812
- hidden_in: bfloat16 [32, 1536, 16384], P('dp', 'ctx'), may hold values from -6 to 6
- doc_lengths: int32 [32, 8], P('dp'), may hold values from 1 to 576, 1536 in all within a row
- span_order: int32 [16], replicated, may hold values from 0 to 15, each once
- m_codes: int32 [16384, 256], P('dp'), may hold values from -127 to 127
- m_scales: float32 [2048], P('dp'), may hold values from 0.05 to 0.5
- v_codes: int32 [16384, 256], P('dp'), may hold values from 1 to 255
- v_scales: float32 [2048], P('dp'), may hold values from 0.05 to 1
Outputs:
- dq: bfloat16 [32, 1536, 2048], P('dp', 'ctx')
- update: float32 [16384, 256], P('dp')
- m_norm: float32 [16384, 256], P('dp')
- m_absmax: float32 [2048], P('dp')
- v_norm: float32 [16384, 256], P('dp')
- v_absmax: float32 [2048], P('dp')
Inputs may be any that keep to these rules, and one draw needn't show every extreme that they name: `doc_lengths`: each sequence's 8 lengths sum to 1536. `span_order`: each stored block names a different position block.
All inputs are finite; a program needn't handle non-finite values. Where the computation divides by a largest or mean magnitude, that divisor is 1e-20 or more.
Results may differ from a plain program's by a relative error of at most 0.0078.
Values may be sent and summed in bfloat16 or wider, within the bound.
A program may use at most 128 MiB of HBM per device.

v0:
```python
import math
import jax
import jax.numpy as jnp
from jax import lax
from jax.sharding import PartitionSpec as P

BLOCK = 2048
STEP = 10


def positions(order, span, total):
    rows = jnp.arange(total, dtype=jnp.int32)
    slot = rows // span
    match = slot[:, None] == jnp.arange(order.shape[0], dtype=jnp.int32)[None, :]
    first = jnp.sum(jnp.where(match, order[None, :], 0), axis=1)
    return first * span + rows % span


def documents(pos, lengths):
    index = jnp.arange(lengths.shape[0], dtype=jnp.int32)
    ends = jnp.sum(jnp.where(index[None, :] <= index[:, None], lengths[None, :], 0), axis=1)
    return jnp.sum((pos[:, None] >= ends[None, :]).astype(jnp.int32), axis=1)


def adam_blocks(grad, m_codes, m_scales, v_codes, v_scales):
    shape = grad.shape
    g_blocks = grad.reshape(-1, BLOCK)
    m_old = m_codes.reshape(-1, BLOCK).astype(jnp.float32) / 127.0 * m_scales[:, None]
    v_old = v_codes.reshape(-1, BLOCK).astype(jnp.float32) / 255.0 * v_scales[:, None]
    moment = 0.9 * m_old + 0.1 * g_blocks
    second = 0.95 * v_old + 0.05 * g_blocks * g_blocks
    update = moment / (1.0 - 0.9**STEP) / (jnp.sqrt(second / (1.0 - 0.95**STEP)) + 1e-08)
    m_absmax = jnp.max(jnp.abs(moment), axis=1)
    v_absmax = jnp.max(second, axis=1)
    m_norm = moment / (m_absmax[:, None] + 1e-06)
    v_norm = second / (v_absmax[:, None] + 1e-06)
    return (update.reshape(shape), m_norm.reshape(shape), m_absmax, v_norm.reshape(shape), v_absmax)


def contract_rows(left, right):
    return lax.dot_general(
        left, right, (((0,), (0,)), ((), ())), preferred_element_type=jnp.float32
    )


def contract_cols(left, right):
    return lax.dot_general(
        left, right, (((1,), (1,)), ((), ())), preferred_element_type=jnp.float32
    )


def shards(
    q_heads,
    keys,
    values,
    out_grad,
    hidden_in,
    doc_lengths,
    span_order,
    m_codes,
    m_scales,
    v_codes,
    v_scales,
):
    rows = q_heads.shape[1]
    head_dim = keys.shape[2]
    heads_width = q_heads.shape[2]
    nheads = heads_width // head_dim
    scale = 1.0 / math.sqrt(head_dim)
    total = rows * lax.axis_size("ctx")
    key_all, value_all = (
        lax.all_gather(keys[0], "ctx", axis=0, tiled=True),
        lax.all_gather(values[0], "ctx", axis=0, tiled=True),
    )
    pos = positions(span_order, rows // 2, total)
    doc = documents(pos, doc_lengths[0])
    first_row = lax.axis_index("ctx") * rows
    query_pos = lax.dynamic_slice_in_dim(pos, first_row, rows)
    query_doc = lax.dynamic_slice_in_dim(doc, first_row, rows)
    queries = q_heads[0].reshape(rows * nheads, head_dim)
    grads_out = out_grad[0].reshape(rows * nheads, head_dim)
    width = min(512, total)
    nblocks = total // width
    blocks = (
        key_all.reshape(nblocks, width, head_dim),
        value_all.reshape(nblocks, width, head_dim),
        pos.reshape(nblocks, width),
        doc.reshape(nblocks, width),
    )

    def block_masks(key_pos, key_doc):
        small = (key_pos[None, :] <= query_pos[:, None]) & (key_doc[None, :] == query_doc[:, None])
        wide = jnp.broadcast_to(small[:, None, :], (rows, nheads, width)).reshape(
            rows * nheads, width
        )
        return (small, wide)

    def forward_terms(carry, block):
        key_block, value_block, key_pos, key_doc = block
        small, wide = block_masks(key_pos, key_doc)
        top, denom, weighted = carry
        scores = contract_cols(queries, key_block) * scale
        dprob = contract_cols(grads_out, value_block)
        new_top = jnp.maximum(top, jnp.max(jnp.where(wide, scores, -1e30), axis=1, keepdims=True))
        expo = jnp.where(wide, jnp.exp(scores - new_top), 0.0)
        factor = jnp.exp(top - new_top)
        result = (
            new_top,
            denom * factor + jnp.sum(expo, axis=1, keepdims=True),
            weighted * factor + jnp.sum(expo * dprob, axis=1, keepdims=True),
        )
        return (result, None)

    column = jnp.zeros((rows * nheads, 1), jnp.float32)
    start_state = (column - 1e30, column, column)
    (top, denom, weighted), unused = lax.scan(forward_terms, start_state, blocks)
    delta = weighted / denom

    def backward_terms(accum, block):
        key_block, value_block, key_pos, key_doc = block
        small, wide = block_masks(key_pos, key_doc)
        acc = accum
        scores = contract_cols(queries, key_block) * scale
        dprob = contract_cols(grads_out, value_block)
        prob = jnp.where(wide, jnp.exp(scores - top), 0.0) / denom
        prob_low = prob.astype(jnp.bfloat16)
        dscore = (prob * (dprob - delta)).astype(jnp.bfloat16)
        acc = acc + jnp.dot(dscore, key_block, preferred_element_type=jnp.float32)
        dkey = contract_rows(dscore, queries) * scale
        dvalue = contract_rows(prob_low, grads_out)
        return (acc, jnp.concatenate([dkey, dvalue], axis=1))

    dq_sum, pieces = lax.scan(
        backward_terms, jnp.zeros((rows * nheads, head_dim), jnp.float32), blocks
    )
    dq = (dq_sum * scale).reshape(1, rows, heads_width).astype(jnp.bfloat16)
    partial_grads = pieces.reshape(total, 2 * head_dim)
    own = lax.psum_scatter(partial_grads, "ctx", scatter_dimension=0, tiled=True)
    own_low = own.astype(jnp.bfloat16)
    layer_in = hidden_in[0]
    grad = lax.psum_scatter(contract_rows(layer_in, own_low), "dp", scatter_dimension=0, tiled=True)
    grad = lax.psum(grad, "ctx")
    update, m_norm, m_absmax, v_norm, v_absmax = adam_blocks(
        grad, m_codes, m_scales, v_codes, v_scales
    )
    return (dq, update, m_norm, m_absmax, v_norm, v_absmax)


def solution(mesh):
    in_specs = (
        P("dp", "ctx", None),
        P("dp", "ctx", None),
        P("dp", "ctx", None),
        P("dp", "ctx", None),
        P("dp", "ctx", None),
        P("dp", None),
        P(),
        P("dp", None),
        P("dp"),
        P("dp", None),
        P("dp"),
    )
    out_specs = (
        P("dp", "ctx", None),
        P("dp", None),
        P("dp", None),
        P("dp"),
        P("dp", None),
        P("dp"),
    )
    return jax.shard_map(shards, mesh=mesh, in_specs=in_specs, out_specs=out_specs, check_vma=False)
```

profile of v0, /device:TPU:32, one launch (start us, length us, event | category | flops | bytes accessed | tf_op | source)
XLA Modules:
  0.0 549.0 jit_solution(25946978486925844)
XLA Ops:
  10.9 29.1 %all-gather = bf16[1,1536,128]{2,1,0:T(8,128)(2,1)S(1)} all-gather(bf16[1,192,128]{2,1,0:T(8,128)(2,1)} %param.16), channel_id=2, replica_groups=mesh['dp'=32,'ctx'=8] {'ctx'}, dimensions={1}, use_global_device_ids=true | all-gather | bytes 442368 | tf_op jit(solution)/shard_map/all_gather | solution.py:72
  41.5 30.8 %all-gather.1 = bf16[1,1536,128]{2,1,0:T(8,128)(2,1)} all-gather(bf16[1,192,128]{2,1,0:T(8,128)(2,1)} %param.17), channel_id=3, replica_groups=mesh['dp'=32,'ctx'=8] {'ctx'}, dimensions={1}, use_global_device_ids=true | all-gather | bytes 442368 | tf_op jit(solution)/shard_map/all_gather | solution.py:73
  72.7 46.8 %while.28 = (s32[]{:T(128)}, f32[3072,1]{0,1:T(1,128)}, f32[3072,1]{0,1:T(1,128)}, f32[3072,1]{0,1:T(1,128)}, s32[3,512]{1,0:T(4,128)}, /*index=5*/s32[192]{0:T(...) while((s32[]{:T(128)}, f32[3072,1]{0,1:T(1,128)}, ...), condition=%wide.region_7.8_spmd.clone, body=%wide.region_3.7_spmd.clone.sunk | while | flops 824497152 | bytes 55990092 | solution.py:116
  74.6 1.7 copy.45
  76.3 3.9 fusion.79
  80.2 5.2 fusion.81
  89.8 1.7 copy.45
  91.5 3.9 fusion.79
  96.0 5.2 fusion.81
  105.6 1.7 copy.45
  107.3 3.8 fusion.79
  111.9 5.2 fusion.81
  120.8 55.8 %while.29 = (s32[]{:T(128)}, f32[3072,128]{1,0:T(8,128)}, f32[3,512,256]{2,1,0:T(8,128)}, s32[3,512]{1,0:T(4,128)}, s32[192]{0:T(256)S(1)}, /*index=5*/s32[3,512...) while((s32[]{:T(128)}, f32[3072,128]{1,0:T(8,128)}, ...), condition=%wide.region_9.10_spmd.clone, body=%wide.region_8.9_spmd.clone.sunk | while | flops 2027126784 | bytes 108267456 | solution.py:133
  124.6 1.9 fusion.94
  126.6 2.9 fusion.95
  129.6 2.2 convolution_add_fusion.2
  132.9 2.3 fusion.96
  135.3 2.3 convolution_multiply_fusion.2
  143.0 1.9 fusion.94
  145.0 2.9 fusion.95
  147.9 3.8 convolution_add_fusion.2
  151.7 2.3 fusion.96
  154.0 2.3 convolution_multiply_fusion.2
  161.7 1.9 fusion.94
  163.7 2.9 fusion.95
  166.6 3.8 convolution_add_fusion.2
  170.4 2.3 fusion.96
  172.7 2.3 convolution_multiply_fusion.2
  176.7 49.4 %reduce-scatter.3.cloned.1.call-done = f32[192,256]{1,0:T(8,128)} async-done(((f32[1536,256]{1,0:T(8,128)}), f32[192,256]{1,0:T(8,128)}) %reduce-scatter.3.cloned.1.call-update) | async-done | bytes 196624 | tf_op jit(solution)/shard_map/reduce_scatter | solution.py:138
  226.1 11.0 %convolution_bitcast_fusion = f32[16384,256]{0,1:T(8,128)} fusion(bf16[1,192,16384]{2,1,0:T(8,128)(2,1)} %param.19, f32[192,256]{1,0:T(8,128)} %reduce-scatter.3.cloned.1.call-done), kind=kOutput, calls=%fused_computation.49 | convolution fusion | flops 1610661888 | bytes 23265280 | tf_op jit(solution)/shard_map/dot_general | solution.py:41
  237.2 218.4 %reduce-scatter.5.cloned.1.call-done = f32[512,256]{0,1:T(8,128)} async-done(((f32[16384,256]{0,1:T(8,128)}), f32[512,256]{0,1:T(8,128)}) %reduce-scatter.5.cloned.1.call-update) | async-done | bytes 524304 | tf_op jit(solution)/shard_map/reduce_scatter | solution.py:141
  457.8 79.3 %all-reduce.2.cloned.1.call-done = f32[512,256]{0,1:T(8,128)} async-done(((f32[512,256]{0,1:T(8,128)}), f32[512,256]{0,1:T(8,128)}) %all-reduce.2.cloned.1.call-update) | async-done | bytes 524304 | tf_op jit(solution)/shard_map/psum | solution.py:142
  (197 shorter events, 45.8 us)
Async XLA Ops:
  7.2 65.1 %copy-start.10 = (bf16[1,192,2048]{2,1,0:T(8,128)(2,1)S(1)}, bf16[1,192,2048]{2,1,0:T(8,128)(2,1)}, u32[]{:S(2)}) copy-start(bf16[1,192,2048]{2,1,0:T(8,128)(2,1)} %param.18) | copy-start | bytes 2359300
  7.2 218.9 %reduce-scatter.3.cloned.1.call-start = ((), (), s32[]{:S(2)}) async-start(), calls=%async_computation.2 | async-start | bytes 1769472 | tf_op jit(solution)/shard_map/reduce_scatter | solution.py:138
  80.2 5.2 copy-start
  96.0 5.2 copy-start
  111.9 5.2 copy-start
  120.8 5.8 %copy-start.4 = (bf16[3072,128]{1,0:T(8,128)(2,1)}, bf16[3072,128]{1,0:T(8,128)(2,1)S(1)}, u32[]{:S(2)}) copy-start(bf16[3072,128]{1,0:T(8,128)(2,1)S(1)} %get-tuple-element.577) | copy-start | bytes 2359300 | tf_op jit(solution)/shard_map/while
  120.8 5.8 %copy-start.6 = (bf16[3072,128]{1,0:T(8,128)(2,1)}, bf16[3072,128]{1,0:T(8,128)(2,1)S(1)}, u32[]{:S(2)}) copy-start(bf16[3072,128]{1,0:T(8,128)(2,1)S(1)} %get-tuple-element.581) | copy-start | bytes 2359300 | tf_op jit(solution)/shard_map/while
  120.8 3.8 copy-start.9
  120.8 3.8 copy-start.16
  126.6 3.0 copy-start.1
  129.6 3.4 copy-start.2
  139.1 5.8 %copy-start.4 = (bf16[3072,128]{1,0:T(8,128)(2,1)}, bf16[3072,128]{1,0:T(8,128)(2,1)S(1)}, u32[]{:S(2)}) copy-start(bf16[3072,128]{1,0:T(8,128)(2,1)S(1)} %get-tuple-element.577) | copy-start | bytes 2359300 | tf_op jit(solution)/shard_map/while
  139.1 5.8 %copy-start.6 = (bf16[3072,128]{1,0:T(8,128)(2,1)}, bf16[3072,128]{1,0:T(8,128)(2,1)S(1)}, u32[]{:S(2)}) copy-start(bf16[3072,128]{1,0:T(8,128)(2,1)S(1)} %get-tuple-element.581) | copy-start | bytes 2359300 | tf_op jit(solution)/shard_map/while
  139.1 3.8 copy-start.9
  139.1 3.8 copy-start.16
  144.9 3.0 copy-start.1
  147.9 3.8 copy-start.2
  157.9 5.8 %copy-start.4 = (bf16[3072,128]{1,0:T(8,128)(2,1)}, bf16[3072,128]{1,0:T(8,128)(2,1)S(1)}, u32[]{:S(2)}) copy-start(bf16[3072,128]{1,0:T(8,128)(2,1)S(1)} %get-tuple-element.577) | copy-start | bytes 2359300 | tf_op jit(solution)/shard_map/while
  157.9 5.8 %copy-start.6 = (bf16[3072,128]{1,0:T(8,128)(2,1)}, bf16[3072,128]{1,0:T(8,128)(2,1)S(1)}, u32[]{:S(2)}) copy-start(bf16[3072,128]{1,0:T(8,128)(2,1)S(1)} %get-tuple-element.581) | copy-start | bytes 2359300 | tf_op jit(solution)/shard_map/while
  157.9 3.8 copy-start.9
  157.9 3.8 copy-start.16
  163.7 3.0 copy-start.1
  166.6 3.8 copy-start.2
  176.6 279.0 %reduce-scatter.5.cloned.1.call-start = ((), (), s32[]{:S(2)}) async-start(), calls=%async_computation.3 | async-start | bytes 17301504 | tf_op jit(solution)/shard_map/reduce_scatter | solution.py:141
  237.1 218.6 %copy-start.3 = (f32[3072,128]{1,0:T(8,128)S(1)}, f32[3072,128]{1,0:T(8,128)}, u32[]{:S(2)}) copy-start(f32[3072,128]{1,0:T(8,128)} %get-tuple-element.146) | copy-start | bytes 4718596
  237.1 219.9 %copy-start.21 = (f32[64]{0:T(128)S(1)}, f32[64]{0:T(128)}, u32[]{:S(2)}) copy-start(f32[64]{0:T(128)} %param.23) | copy-start | bytes 772
  237.2 220.1 %copy-start.11 = (s32[512,256]{1,0:T(8,128)S(1)}, s32[512,256]{1,0:T(8,128)}, u32[]{:S(2)}) copy-start(s32[512,256]{1,0:T(8,128)} %param.22) | copy-start | bytes 1572868
  237.2 220.3 %copy-start.22 = (f32[64]{0:T(128)S(1)}, f32[64]{0:T(128)}, u32[]{:S(2)}) copy-start(f32[64]{0:T(128)} %param.25) | copy-start | bytes 772
  237.2 220.4 %copy-start.12 = (s32[512,256]{1,0:T(8,128)S(1)}, s32[512,256]{1,0:T(8,128)}, u32[]{:S(2)}) copy-start(s32[512,256]{1,0:T(8,128)} %param.24) | copy-start | bytes 1572868
  237.2 300.0 %all-reduce.2.cloned.1.call-start = ((), (), s32[]{:S(2)}) async-start(), calls=%async_computation.4 | async-start | bytes 1048576 | tf_op jit(solution)/shard_map/psum | solution.py:142
  538.6 3.9 copy-start.19
  539.0 3.5 copy-start.20
  (24 other events, 33.0 us)
Sparse Core Ops, SparseCore 0:
  176.7 49.3 reduce-scatter.2
  237.3 218.3 reduce-scatter.4
  458.5 78.6 all-reduce.1
where the time goes:
time: 550 us; the launch traced here: 549 us
  waiting for transfers between devices  347 us (63%)
  matrix products  76.2 us (14%)
  blocking collectives  59.9 us (11%)
  local copies, waits for them, and re-layouts  33.6 us (6%)
  other arithmetic  17.1 us (3%)
  between operations  14 us (3%)
    reduce_scatter x1, waiting for transfers between devices, shards(): lax.psum_scatter(contract_rows(layer_in, own_low), 'dp', scatter_dimensio...  218 us
    psum x1, waiting for transfers between devices, shards(): grad = lax.psum(grad, 'ctx')  79.3 us
    reduce_scatter x1, waiting for transfers between devices, shards(): lax.psum_scatter(partial_grads, 'ctx', scatter_dimension=0, tiled=True)  49.4 us
    dot_general x12, matrix products, contract_cols(): lax.dot_general(left, right, (((1,), (1,)), ((), ())), preferred_element_...  41.6 us
    all_gather x1, blocking collectives, shards(): lax.all_gather(values[0], 'ctx', axis=0, tiled=True)  30.8 us
    all_gather x1, blocking collectives, shards(): lax.all_gather(keys[0], 'ctx', axis=0, tiled=True)  29.1 us
    dot_general x7, matrix products, contract_rows(): lax.dot_general(left, right, (((0,), (0,)), ((), ())), preferred_element_...  24.8 us
  transfers between devices with their start and end apart: 3, of which 3 were waited for; matrix products, arithmetic and copies ran while one was open for 0% of the time, Pallas kernels for 0%

commit v1 on v0

--- a/solution.py
+++ b/solution.py
@@ -139,7 +139,8 @@
     own_low = own.astype(jnp.bfloat16)
     layer_in = hidden_in[0]
     grad = lax.psum_scatter(contract_rows(layer_in, own_low), "dp", scatter_dimension=0, tiled=True)
-    grad = lax.psum(grad, "ctx")
+    plain = lax.all_gather(grad, axis_name="ctx")
+    grad = jnp.sum(plain, axis=0)
     update, m_norm, m_absmax, v_norm, v_absmax = adam_blocks(
         grad, m_codes, m_scales, v_codes, v_scales
     )

time: 550 us -> 578 us (1.051)
  waiting for transfers between devices: 347 us -> 358 us
  matrix products: 76.2 us -> 83.3 us
  local copies, waits for them, and re-layouts: 33.6 us -> 39.5 us
    all_gather x0 -> x1, waiting for transfers between devices: none -> 90.1 us  [shards(): plain = lax.all_gather(grad, axis_name='ctx')]
    psum x1 -> x0, waiting for transfers between devices: 79.3 us -> none  [shards(): grad = lax.psum(grad, 'ctx')]
    dot_general x12, matrix products: 41.6 us -> 48.8 us  [contract_cols(): lax.dot_general(left, right, (((1,), (1,)), ((), ())), preferred_element_...]
    unnamed x21 -> x18, local copies, waits for them, and re-layouts: 3.42 us -> 10.4 us
  transfers between devices with their start and end apart: 3 -> 3, of which waited for: 3 -> 3; matrix products, arithmetic and copies ran while one was open for 0% -> 1% of each run, Pallas kernels for 0% -> 0%
where the time goes in v1:
time: 578 us; the launch traced here: 574 us
  waiting for transfers between devices  358 us (62%)
  matrix products  83.3 us (14%)
  blocking collectives  59.9 us (10%)
  local copies, waits for them, and re-layouts  39.5 us (7%)
  other arithmetic  18.8 us (3%)
  between operations  14 us (2%)
    reduce_scatter x1, waiting for transfers between devices, shards(): lax.psum_scatter(contract_rows(layer_in, own_low), 'dp', scatter_dimensio...  219 us
    all_gather x1, waiting for transfers between devices, shards(): plain = lax.all_gather(grad, axis_name='ctx')  90.1 us
    reduce_scatter x1, waiting for transfers between devices, shards(): lax.psum_scatter(partial_grads, 'ctx', scatter_dimension=0, tiled=True)  49.2 us
    dot_general x12, matrix products, contract_cols(): lax.dot_general(left, right, (((1,), (1,)), ((), ())), preferred_element_...  48.8 us
    all_gather x1, blocking collectives, shards(): lax.all_gather(values[0], 'ctx', axis=0, tiled=True)  30.8 us
    all_gather x1, blocking collectives, shards(): lax.all_gather(keys[0], 'ctx', axis=0, tiled=True)  29.1 us
    dot_general x7, matrix products, contract_rows(): lax.dot_general(left, right, (((0,), (0,)), ((), ())), preferred_element_...  24.8 us
  transfers between devices with their start and end apart: 3, of which 3 were waited for; matrix products, arithmetic and copies ran while one was open for 1% of the time, Pallas kernels for 0%

profile of v1, /device:TPU:32, one launch (start us, length us, event | category | flops | bytes accessed | tf_op | source)
XLA Modules:
  0.0 574.2 jit_solution(13586583594535981172)
XLA Ops:
  10.9 29.1 %all-gather = bf16[1,1536,128]{2,1,0:T(8,128)(2,1)S(1)} all-gather(bf16[1,192,128]{2,1,0:T(8,128)(2,1)} %param.16), channel_id=2, replica_groups=mesh['dp'=32,'ctx'=8] {'ctx'}, dimensions={1}, use_global_device_ids=true | all-gather | bytes 442368 | tf_op jit(solution)/shard_map/all_gather | solution.py:72
  39.9 2.2 reshape_squeeze.6
  42.1 30.8 %all-gather.1 = bf16[1,1536,128]{2,1,0:T(8,128)(2,1)} all-gather(bf16[1,192,128]{2,1,0:T(8,128)(2,1)} %param.17), channel_id=3, replica_groups=mesh['dp'=32,'ctx'=8] {'ctx'}, dimensions={1}, use_global_device_ids=true | all-gather | bytes 442368 | tf_op jit(solution)/shard_map/all_gather | solution.py:73
  72.9 2.2 reshape_squeeze.7
  75.2 50.5 %while.28 = (s32[]{:T(128)}, f32[3072,1]{0,1:T(1,128)S(1)}, f32[3072,1]{0,1:T(1,128)}, f32[3072,1]{0,1:T(1,128)S(1)}, s32[3,512]{1,0:T(4,128)}, /*index=5*/s32[1...) while((s32[]{:T(128)}, f32[3072,1]{0,1:T(1,128)S(1)}, ...), condition=%wide.region_7.8_spmd.clone, body=%wide.region_3.7_spmd.clone.sunk | while | flops 824497152 | bytes 55744192 | solution.py:116
  78.8 5.0 fusion.79
  83.9 5.4 fusion.81
  95.2 5.0 fusion.79
  100.2 5.3 fusion.81
  112.3 5.0 fusion.79
  117.3 5.4 fusion.81
  127.0 56.8 %while.29 = (s32[]{:T(128)}, f32[3072,128]{1,0:T(8,128)}, f32[3,512,256]{2,1,0:T(8,128)}, s32[3,512]{1,0:T(4,128)}, s32[192]{0:T(256)S(1)}, /*index=5*/s32[3,512...) while((s32[]{:T(128)}, f32[3072,128]{1,0:T(8,128)}, ...), condition=%wide.region_9.10_spmd.clone, body=%wide.region_8.9_spmd.clone.sunk | while | flops 2027126784 | bytes 95536888 | solution.py:133
  130.7 3.1 fusion.94
  133.8 2.8 fusion.95
  136.6 2.2 convolution_add_fusion.2
  140.0 2.3 fusion.96
  142.3 2.3 convolution_multiply_fusion.2
  149.4 3.1 fusion.94
  152.5 2.8 fusion.95
  155.3 3.7 convolution_add_fusion.2
  159.1 2.3 fusion.96
  161.4 2.3 convolution_multiply_fusion.2
  168.5 3.1 fusion.94
  171.6 2.8 fusion.95
  174.4 3.7 convolution_add_fusion.2
  178.1 2.3 fusion.96
  180.5 2.3 convolution_multiply_fusion.2
  183.9 49.2 %reduce-scatter.3.cloned.1.call-done = f32[192,256]{1,0:T(8,128)} async-done(((f32[1536,256]{1,0:T(8,128)}), f32[192,256]{1,0:T(8,128)}) %reduce-scatter.3.cloned.1.call-update) | async-done | bytes 196624 | tf_op jit(solution)/shard_map/reduce_scatter | solution.py:138
  233.1 11.0 %convolution_bitcast_fusion = f32[16384,256]{0,1:T(8,128)} fusion(bf16[1,192,16384]{2,1,0:T(8,128)(2,1)} %param.19, f32[192,256]{1,0:T(8,128)} %reduce-scatter.3.cloned.1.call-done), kind=kOutput, calls=%fused_computation.49 | convolution fusion | flops 1610661888 | bytes 23265280 | tf_op jit(solution)/shard_map/dot_general | solution.py:41
  244.4 218.7 %reduce-scatter.5.cloned.1.call-done = f32[512,256]{0,1:T(8,128)} async-done(((f32[16384,256]{0,1:T(8,128)}), f32[512,256]{0,1:T(8,128)}) %reduce-scatter.5.cloned.1.call-update) | async-done | bytes 524304 | tf_op jit(solution)/shard_map/reduce_scatter | solution.py:141
  466.3 90.1 %all-gather.5.cloned.1.call-done = f32[4096,256]{0,1:T(8,128)} async-done(((f32[512,256]{0,1:T(8,128)}), f32[4096,256]{0,1:T(8,128)}) %all-gather.5.cloned.1.call-update) | async-done | bytes 4194320 | tf_op jit(solution)/shard_map/all_gather | solution.py:142
  556.4 6.0 %copy.42 = f32[32,8,8,512]{3,2,1,0:T(8,128)S(1)} copy(f32[32,8,8,512]{3,1,2,0:T(8,128)} %bitcast.149) | data formatting | bytes 8388608
  (123 shorter events, 48.3 us)
Async XLA Ops:
  7.2 225.9 %reduce-scatter.3.cloned.1.call-start = ((), (), s32[]{:S(2)}) async-start(), calls=%async_computation.2 | async-start | bytes 1769472 | tf_op jit(solution)/shard_map/reduce_scatter | solution.py:138
  83.8 5.4 copy-start
  100.2 5.4 copy-start
  117.3 5.4 copy-start
  133.8 2.8 copy-start.1
  136.6 3.4 copy-start.2
  152.5 2.8 copy-start.1
  155.3 3.8 copy-start.2
  171.5 2.8 copy-start.1
  174.4 3.8 copy-start.2
  183.9 279.3 %reduce-scatter.5.cloned.1.call-start = ((), (), s32[]{:S(2)}) async-start(), calls=%async_computation.3 | async-start | bytes 17301504 | tf_op jit(solution)/shard_map/reduce_scatter | solution.py:141
  244.1 219.1 %copy-start.3 = (f32[3072,128]{1,0:T(8,128)S(1)}, f32[3072,128]{1,0:T(8,128)}, u32[]{:S(2)}) copy-start(f32[3072,128]{1,0:T(8,128)} %get-tuple-element.146) | copy-start | bytes 4718596
  244.1 220.4 %copy-start.7 = (f32[64]{0:T(128)S(1)}, f32[64]{0:T(128)}, u32[]{:S(2)}) copy-start(f32[64]{0:T(128)} %param.23) | copy-start | bytes 772
  244.1 220.6 %copy-start.4 = (s32[512,256]{1,0:T(8,128)S(1)}, s32[512,256]{1,0:T(8,128)}, u32[]{:S(2)}) copy-start(s32[512,256]{1,0:T(8,128)} %param.22) | copy-start | bytes 1572868
  244.1 220.8 %copy-start.8 = (f32[64]{0:T(128)S(1)}, f32[64]{0:T(128)}, u32[]{:S(2)}) copy-start(f32[64]{0:T(128)} %param.25) | copy-start | bytes 772
  244.2 312.3 %all-gather.5.cloned.1.call-start = ((), (), s32[]{:S(2)}) async-start(), calls=%async_computation.4 | async-start | bytes 4718592 | tf_op jit(solution)/shard_map/all_gather | solution.py:142
  563.8 3.9 copy-start.5
  564.2 3.5 copy-start.6
Sparse Core Ops, SparseCore 0:
  184.0 49.0 reduce-scatter.2
  244.2 218.8 reduce-scatter.4
  465.1 91.2 all-gather.4
